TPU v7x, 32 devices: a whole 2x2x4 slice. The times are simulated.
32 devices in a mesh: clips: 2 (over y), tm: 4 (over x, core), rows: 4 (over z).
Axes of the slice: x: 2, y: 2, z: 4, core: 2. Of those that a mesh axis runs over, the one named last changes fastest.
Arguments:
- features: bfloat16 [8, 8, 48, 384], P(('clips', 'tm'), 'rows'), parts along dimension 0, may hold values from -320 to 320
- first_gain: float32 [384], replicated, may hold values from 0.5 to 1.5
- first_shift: float32 [384], replicated, may hold values from -3 to 3
- first_kernel: bfloat16 [384, 3, 3, 3, 384], P('tm'), may hold values from -0.0625 to 0.0625
- first_bias: float32 [384], P('tm'), may hold values from -2 to 2
- second_gain: float32 [384], replicated, may hold values from 0.5 to 1.5
- second_shift: float32 [384], replicated, may hold values from -3 to 3
- second_kernel: bfloat16 [384, 3, 3, 3, 384], P('tm'), may hold values from -0.0625 to 0.0625
- second_bias: float32 [384], P('tm'), may hold values from -2 to 2
- third_gain: float32 [384], replicated, may hold values from 0.5 to 1.5
- third_shift: float32 [384], replicated, may hold values from -3 to 3
- query_weight: bfloat16 [384, 384], replicated, may hold values from -0.30618622 to 0.30618622
- key_weight: bfloat16 [384, 384], replicated, may hold values from -1.8371173 to 1.8371173
- value_weight: bfloat16 [384, 384], replicated, may hold values from -0.3125 to 0.3125
- output_weight: bfloat16 [384, 384], replicated, may hold values from -0.3125 to 0.3125
Outputs:
- decoded: bfloat16 [8, 8, 48, 384], P(('clips', 'tm'), 'rows'), parts along dimension 0
There are 2 independent parts, one for each index of `clips`. A program takes and returns all parts, laid end to end along the dimension named above; an argument that names none is the same for every part. Nothing has to cross between parts.
All inputs are finite; a program needn't handle non-finite values.
Results may differ from a plain program's by a relative error of at most 0.029.
Values may be sent and summed in bfloat16 or wider, within the bound.
A program may use at most 64 MiB of HBM per device.

v0:
```python
import jax
import jax.numpy as jnp
from jax import lax
from jax.sharding import PartitionSpec as P

C = 384
GROUPS = 32
epsilon = 1e-06


def extended(cells, sides, width):
    for axis, dim in sides:
        count = lax.axis_size(axis)
        ends = count - 1
        head = lax.slice_in_dim(cells, 0, width, axis=dim)
        tail = lax.slice_in_dim(cells, cells.shape[dim] - width, cells.shape[dim], axis=dim)
        cells = jnp.concatenate(
            [
                lax.ppermute(tail, axis, [(i, (i + 1) % count) for i in range(ends)]),
                cells,
                lax.ppermute(head, axis, [((i + 1) % count, i) for i in range(ends)]),
            ],
            axis=dim,
        )
    return cells


def group_norm(values, gain, shift):
    frame_count, row_count, col_count, channels = values.shape
    entries = lax.axis_size("rows") * row_count * col_count * (channels // GROUPS)
    grouped = values.reshape(frame_count, row_count, col_count, GROUPS, channels // GROUPS)
    sums = lax.psum(jnp.sum(grouped, axis=(1, 2, 4)), "rows")
    average = sums / entries
    centered = grouped - average[:, None, None, :, None]
    variance = lax.psum(jnp.sum(centered * centered, axis=(1, 2, 4)), "rows") / entries
    scaled = centered * lax.rsqrt(variance + epsilon)[:, None, None, :, None]
    return scaled.reshape(frame_count, row_count, col_count, channels) * gain + shift


def causal_conv(active, kernel, bias):
    widened = extended(active, (("rows", 1),), 1)
    clip_frames = lax.all_gather(widened, "tm", axis=0, tiled=True)
    frame_count, padded_rows, col_count, channels = clip_frames.shape
    row_count = padded_rows - 2
    outputs = kernel.shape[0]
    padded = jnp.pad(clip_frames, ((2, 0), (0, 0), (1, 1), (0, 0)))
    summed = jnp.zeros((outputs, frame_count * row_count * col_count), jnp.float32)
    for tap_time in range(3):
        for tap_row in range(3):
            window = padded[tap_time : tap_time + frame_count, tap_row : tap_row + row_count]
            stacked = jnp.concatenate(
                [window[:, :, shift_col : shift_col + col_count] for shift_col in range(3)], axis=-1
            )
            tap_weight = kernel[:, tap_time, tap_row].reshape(outputs, 3 * channels)
            summed = summed + lax.dot_general(
                tap_weight,
                stacked.reshape(-1, 3 * channels),
                (((1,), (1,)), ((), ())),
                preferred_element_type=jnp.float32,
            )
    result = (
        (summed + bias[:, None])
        .astype(jnp.bfloat16)
        .reshape(outputs, frame_count, row_count, col_count)
    )
    mixed = lax.all_to_all(result, "tm", split_axis=1, concat_axis=0, tiled=True)
    return jnp.transpose(mixed, (1, 2, 3, 0))


def absorb(carry, queries, keys, values):
    peak, total, summed = carry
    scores = jnp.einsum("fqc,fkc->fqk", queries, keys, preferred_element_type=jnp.float32)
    new_peak = jnp.max(scores, axis=-1)
    factor = jnp.exp(peak - new_peak)
    expon = jnp.exp(scores - new_peak[..., None])
    total = total * factor + jnp.sum(expon, axis=-1)
    summed = summed * factor[..., None] + jnp.einsum(
        "fqk,fkc->fqc", expon.astype(jnp.bfloat16), values, preferred_element_type=jnp.float32
    )
    return (new_peak, total, summed)


def per_device(
    features,
    first_gain,
    first_shift,
    first_kernel,
    first_bias,
    second_gain,
    second_shift,
    second_kernel,
    second_bias,
    third_gain,
    third_shift,
    query_weight,
    key_weight,
    value_weight,
    output_weight,
):
    frame_count, row_count, col_count, channels = features.shape
    start = features.astype(jnp.float32)
    active1 = jax.nn.silu(group_norm(start, first_gain, first_shift)).astype(jnp.bfloat16)
    conv1 = causal_conv(active1, first_kernel, first_bias)
    active2 = jax.nn.silu(group_norm(conv1.astype(jnp.float32), second_gain, second_shift)).astype(
        jnp.bfloat16
    )
    conv2 = causal_conv(active2, second_kernel, second_bias)
    hidden = (start + conv2.astype(jnp.float32)).astype(jnp.bfloat16)
    normed = group_norm(hidden.astype(jnp.float32), third_gain, third_shift).astype(jnp.bfloat16)
    flat = normed.reshape(frame_count, row_count * col_count, channels)
    queries = (
        jnp.einsum("fpc,cd->fpd", flat, query_weight, preferred_element_type=jnp.float32)
        * C ** (-0.5)
    ).astype(jnp.bfloat16)
    positions = row_count * col_count
    initial = (
        jnp.full((frame_count, positions), -jnp.inf, jnp.float32),
        jnp.zeros((frame_count, positions), jnp.float32),
        jnp.zeros((frame_count, positions, channels), jnp.float32),
    )
    keys = jnp.einsum("fpc,cd->fpd", flat, key_weight, preferred_element_type=jnp.float32).astype(
        jnp.bfloat16
    )
    values = jnp.einsum(
        "fpc,cd->fpd", flat, value_weight, preferred_element_type=jnp.float32
    ).astype(jnp.bfloat16)
    shape4 = (frame_count, row_count, col_count, channels)
    peak, total, summed = absorb(
        initial,
        queries,
        lax.all_gather(keys.reshape(shape4), "rows", axis=1, tiled=True).reshape(
            frame_count, -1, channels
        ),
        lax.all_gather(values.reshape(shape4), "rows", axis=1, tiled=True).reshape(
            frame_count, -1, channels
        ),
    )
    attended = (summed / total[..., None]).astype(jnp.bfloat16)
    projected = jnp.einsum(
        "fpc,cd->fpd", attended, output_weight, preferred_element_type=jnp.float32
    )
    decoded = hidden.astype(jnp.float32) + projected.reshape(
        frame_count, row_count, col_count, channels
    )
    return decoded.astype(jnp.bfloat16)


def solution(mesh):
    in_specs = (
        P(("clips", "tm"), "rows", None, None),
        P(),
        P(),
        P("tm", None, None, None, None),
        P("tm"),
        P(),
        P(),
        P("tm", None, None, None, None),
        P("tm"),
        P(),
        P(),
        P(),
        P(),
        P(),
        P(),
    )
    out_specs = P(("clips", "tm"), "rows", None, None)
    return jax.shard_map(
        per_device, mesh=mesh, in_specs=in_specs, out_specs=out_specs, check_vma=False
    )
```

profile of v0, /device:TPU:0, one launch (start us, length us, event | category | flops | bytes accessed | tf_op | source)
XLA Modules:
  0.0 157.3 jit_solution(10581170224222182222)
XLA Ops:
  0.0 1.0 convert_reduce_fusion.1
  1.2 13.5 %psum.42 = f32[1,32]{1,0:T(1,128)S(1)} all-reduce(f32[1,32]{1,0:T(1,128)S(1)} %bitcast.277), channel_id=1, replica_groups=mesh['clips'=2,'tm'=4,'rows'=4] {'rows'}, use_global_device_ids=true, to_apply=%region_2.0 | all-reduce | flops 32 | bytes 256 | tf_op jit(solution)/shard_map/psum | solution.py:32
  14.8 0.9 fusion.21
  16.0 8.4 %psum.43 = f32[1,32]{1,0:T(1,128)S(1)} all-reduce(f32[1,32]{1,0:T(1,128)S(1)} %bitcast.278), channel_id=1, replica_groups=mesh['clips'=2,'tm'=4,'rows'=4] {'rows'}, use_global_device_ids=true, to_apply=%region_5.6 | all-reduce | flops 32 | bytes 256 | tf_op jit(solution)/shard_map/psum | solution.py:35
  24.5 1.0 fusion.29
  25.5 3.9 %collective-permute-start = (bf16[1,1,48,384]{3,2,1,0:T(8,128)(2,1)S(1)}, bf16[1,1,48,384]{3,2,1,0:T(8,128)(2,1)S(1)}, u32[]{:S(2)}, u32[]{:S(2)}) collective-permute-start(bf16[1,1,48,384]{3,2,1,0:T(8,128)(2,1)S(1)} %get-tuple-element.81), channel_id=1, source_target_pairs={{0,1},{1,2},{2,3},{4,5},{5,6},{6,7},{8,9},{9,10},{10,11},{12,13},{... | collective-permute-start | bytes 110600 | tf_op jit(solution)/shard_map/ppermute | solution.py:19
  29.4 1.3 collective-permute-start.1
  30.7 1.8 %fusion.45 = (bf16[96,1,1,3,384]{4,0,3,2,1:T(8,128)(2,1)S(1)}, bf16[96,1,1,3,384]{4,0,3,2,1:T(8,128)(2,1)S(1)}, bf16[96,1,1,3,384]{4,0,3,2,1:T(8,128)(2,1)S(1)},...) fusion(bf16[96,3,3,3,384]{4,0,3,2,1:T(8,128)(2,1)} %param.18), kind=kLoop, calls=%fused_computation.150 | loop fusion | bytes 3981312 | tf_op jit(solution)/shard_map/slice | solution.py:54
  34.3 1.0 collective-permute-done.1
  35.3 7.5 %all_gather.12 = bf16[4,4,48,384]{3,2,1,0:T(8,128)(2,1)S(1)} all-gather(bf16[1,4,48,384]{3,2,1,0:T(8,128)(2,1)S(1)} %pad_maximum_fusion.18), channel_id=1, replica_groups=mesh['clips'=2,'tm'=4,'rows'=4] {'tm'}, dimensions={0}, use_global_device_ids=true | all-gather | bytes 737280 | tf_op jit(solution)/shard_map/all_gather | solution.py:42
  42.8 1.8 %pad_slice_fusion.25 = (bf16[4,2,48,384]{3,2,1,0:T(8,128)(2,1)S(1)}, bf16[4,2,48,384]{3,2,1,0:T(8,128)(2,1)S(1)}, bf16[4,2,48,384]{3,2,1,0:T(8,128)(2,1)S(1)}, b...) fusion(bf16[4,4,48,384]{3,2,1,0:T(8,128)(2,1)S(1)} %all_gather.12), kind=kLoop, calls=%fused_computation.25 | loop fusion | bytes 6193152 | tf_op jit(solution)/shard_map/slice | solution.py:52
  45.5 0.4 convolution_add_fusion.16
  46.1 0.4 convolution_add_fusion.15
  47.1 0.4 convolution_add_fusion.13
  49.7 6.7 %all_to_all.8 = bf16[96,4,2,48]{0,3,2,1:T(8,128)(2,1)S(1)} all-to-all(bf16[96,4,2,48]{0,3,2,1:T(8,128)(2,1)S(1)} %bitcast.270), channel_id=1, replica_groups=mesh['clips'=2,'tm'=4,'rows'=4] {'tm'}, dimensions={1} | all-to-all | bytes 147456 | tf_op jit(solution)/shard_map/all_to_all | solution.py:66
  56.9 10.1 %psum.44 = f32[1,32]{1,0:T(1,128)S(1)} all-reduce(f32[1,32]{1,0:T(1,128)S(1)} %bitcast.279), channel_id=1, replica_groups=mesh['clips'=2,'tm'=4,'rows'=4] {'rows'}, use_global_device_ids=true, to_apply=%region_8.9 | all-reduce | flops 32 | bytes 256 | tf_op jit(solution)/shard_map/psum | solution.py:32
  67.5 8.7 %psum.45 = f32[1,32]{1,0:T(1,128)S(1)} all-reduce(f32[1,32]{1,0:T(1,128)S(1)} %bitcast.280), channel_id=1, replica_groups=mesh['clips'=2,'tm'=4,'rows'=4] {'rows'}, use_global_device_ids=true, to_apply=%region_11.12 | all-reduce | flops 32 | bytes 256 | tf_op jit(solution)/shard_map/psum | solution.py:35
  76.4 3.6 %collective-permute-start.2 = (bf16[1,1,48,384]{3,2,1,0:T(8,128)(2,1)S(1)}, bf16[1,1,48,384]{3,2,1,0:T(8,128)(2,1)S(1)}, u32[]{:S(2)}, u32[]{:S(2)}) collective-permute-start(bf16[1,1,48,384]{3,2,1,0:T(8,128)(2,1)S(1)} %get-tuple-element.79), channel_id=1, source_target_pairs={{0,1},{1,2},{2,3},{4,5},{5,6},{6,7},{8,9},{9,10},{10,11},{12,13},{... | collective-permute-start | bytes 110600 | tf_op jit(solution)/shard_map/ppermute | solution.py:19
  80.0 1.3 collective-permute-start.3
  83.3 2.5 %collective-permute-done.3 = bf16[1,1,48,384]{3,2,1,0:T(8,128)(2,1)S(1)} collective-permute-done((bf16[1,1,48,384]{3,2,1,0:T(8,128)(2,1)S(1)}, bf16[1,1,48,384]{3,2,1,0:T(8,128)(2,1)S(1)}, u32[]{:S(2)}, u32[]{:S(2)}) %collective-permute-start.3) | collective-permute-done | bytes 36896 | tf_op jit(solution)/shard_map/ppermute | solution.py:21
  85.9 6.9 %all_gather.13 = bf16[4,4,48,384]{3,2,1,0:T(8,128)(2,1)S(1)} all-gather(bf16[1,4,48,384]{3,2,1,0:T(8,128)(2,1)S(1)} %pad_maximum_fusion.19), channel_id=1, replica_groups=mesh['clips'=2,'tm'=4,'rows'=4] {'tm'}, dimensions={0}, use_global_device_ids=true | all-gather | bytes 737280 | tf_op jit(solution)/shard_map/all_gather | solution.py:42
  92.8 1.7 %pad_slice_fusion.1 = (bf16[4,2,48,384]{3,2,1,0:T(8,128)(2,1)S(1)}, bf16[4,2,48,384]{3,2,1,0:T(8,128)(2,1)S(1)}, bf16[4,2,48,384]{3,2,1,0:T(8,128)(2,1)S(1)}, bf...) fusion(bf16[4,4,48,384]{3,2,1,0:T(8,128)(2,1)S(1)} %all_gather.13), kind=kLoop, calls=%fused_computation.1 | loop fusion | bytes 6193152 | tf_op jit(solution)/shard_map/slice | solution.py:52
  97.7 0.4 convolution_add_fusion.4
  98.5 0.4 convolution_add_fusion.2
  99.0 0.4 fusion.11
  99.5 6.7 %all_to_all.9 = bf16[96,4,2,48]{0,3,2,1:T(8,128)(2,1)S(1)} all-to-all(bf16[96,4,2,48]{0,3,2,1:T(8,128)(2,1)S(1)} %bitcast.271), channel_id=1, replica_groups=mesh['clips'=2,'tm'=4,'rows'=4] {'tm'}, dimensions={1} | all-to-all | bytes 147456 | tf_op jit(solution)/shard_map/all_to_all | solution.py:66
  106.8 8.5 %psum.46 = f32[1,32]{1,0:T(1,128)S(1)} all-reduce(f32[1,32]{1,0:T(1,128)S(1)} %bitcast.281), channel_id=1, replica_groups=mesh['clips'=2,'tm'=4,'rows'=4] {'rows'}, use_global_device_ids=true, to_apply=%region_14.15 | all-reduce | flops 32 | bytes 256 | tf_op jit(solution)/shard_map/psum | solution.py:32
  115.8 10.2 %psum.47 = f32[1,32]{1,0:T(1,128)S(1)} all-reduce(f32[1,32]{1,0:T(1,128)S(1)} %bitcast.276), channel_id=1, replica_groups=mesh['clips'=2,'tm'=4,'rows'=4] {'rows'}, use_global_device_ids=true, to_apply=%region_17.18 | all-reduce | flops 32 | bytes 256 | tf_op jit(solution)/shard_map/psum | solution.py:35
  126.5 14.7 %all_gather.14 = bf16[1,8,48,384]{3,2,0,1:T(8,128)(2,1)S(1)} all-gather(bf16[1,2,48,384]{3,2,0,1:T(8,128)(2,1)S(1)} %bitcast.274), channel_id=1, replica_groups=mesh['clips'=2,'tm'=4,'rows'=4] {'rows'}, dimensions={1}, use_global_device_ids=true | all-gather | bytes 368640 | tf_op jit(solution)/shard_map/all_gather | solution.py:131
  141.2 0.5 fusion.50
  142.1 14.1 %all_gather.15 = bf16[1,8,48,384]{3,2,0,1:T(8,128)(2,1)S(1)} all-gather(bf16[1,2,48,384]{3,2,0,1:T(8,128)(2,1)S(1)} %bitcast.273), channel_id=1, replica_groups=mesh['clips'=2,'tm'=4,'rows'=4] {'rows'}, dimensions={1}, use_global_device_ids=true | all-gather | bytes 368640 | tf_op jit(solution)/shard_map/all_gather | solution.py:134
  156.4 0.8 fusion.4
  (144 shorter events, 15.0 us)
Async XLA Ops:
  0.0 141.2 %copy-start = (bf16[384,384]{1,0:T(8,128)(2,1)S(1)}, bf16[384,384]{1,0:T(8,128)(2,1)}, u32[]{:S(2)}) copy-start(bf16[384,384]{1,0:T(8,128)(2,1)} %param.26) | copy-start | bytes 884740
  25.5 8.8 %collective-permute-start = (bf16[1,1,48,384]{3,2,1,0:T(8,128)(2,1)S(1)}, bf16[1,1,48,384]{3,2,1,0:T(8,128)(2,1)S(1)}, u32[]{:S(2)}, u32[]{:S(2)}) collective-permute-start(bf16[1,1,48,384]{3,2,1,0:T(8,128)(2,1)S(1)} %get-tuple-element.81), channel_id=1, source_target_pairs={{0,1},{1,2},{2,3},{4,5},{5,6},{6,7},{8,9},{9,10},{10,11},{12,13},{... | collective-permute-start | bytes 110600 | tf_op jit(solution)/shard_map/ppermute | solution.py:19
  29.4 5.9 %collective-permute-start.1 = (bf16[1,1,48,384]{3,2,1,0:T(8,128)(2,1)S(1)}, bf16[1,1,48,384]{3,2,1,0:T(8,128)(2,1)S(1)}, u32[]{:S(2)}, u32[]{:S(2)}) collective-permute-start(bf16[1,1,48,384]{3,2,1,0:T(8,128)(2,1)S(1)} %get-tuple-element.82), channel_id=1, source_target_pairs={{1,0},{2,1},{3,2},{5,4},{6,5},{7,6},{9,8},{10,9},{11,10},{13,12},{... | collective-permute-start | bytes 110600 | tf_op jit(solution)/shard_map/ppermute | solution.py:21
  48.5 0.7 copy-start.10
  49.0 27.3 %copy-start.6 = (f32[384]{0:T(512)S(1)}, f32[384]{0:T(512)}, u32[]{:S(2)}) copy-start(f32[384]{0:T(512)} %param.21) | copy-start | bytes 4612
  49.0 27.3 %copy-start.7 = (f32[384]{0:T(512)S(1)}, f32[384]{0:T(512)}, u32[]{:S(2)}) copy-start(f32[384]{0:T(512)} %param.20) | copy-start | bytes 4612
  49.0 32.3 %copy-start.1 = (bf16[96,3,3,3,384]{4,0,3,2,1:T(8,128)(2,1)S(1)}, bf16[96,3,3,3,384]{4,0,3,2,1:T(8,128)(2,1)}, u32[]{:S(2)}) copy-start(bf16[96,3,3,3,384]{4,0,3,2,1:T(8,128)(2,1)} %param.22) | copy-start | bytes 5971972
  76.4 6.9 %collective-permute-start.2 = (bf16[1,1,48,384]{3,2,1,0:T(8,128)(2,1)S(1)}, bf16[1,1,48,384]{3,2,1,0:T(8,128)(2,1)S(1)}, u32[]{:S(2)}, u32[]{:S(2)}) collective-permute-start(bf16[1,1,48,384]{3,2,1,0:T(8,128)(2,1)S(1)} %get-tuple-element.79), channel_id=1, source_target_pairs={{0,1},{1,2},{2,3},{4,5},{5,6},{6,7},{8,9},{9,10},{10,11},{12,13},{... | collective-permute-start | bytes 110600 | tf_op jit(solution)/shard_map/ppermute | solution.py:19
  80.0 5.9 %collective-permute-start.3 = (bf16[1,1,48,384]{3,2,1,0:T(8,128)(2,1)S(1)}, bf16[1,1,48,384]{3,2,1,0:T(8,128)(2,1)S(1)}, u32[]{:S(2)}, u32[]{:S(2)}) collective-permute-start(bf16[1,1,48,384]{3,2,1,0:T(8,128)(2,1)S(1)} %get-tuple-element.80), channel_id=1, source_target_pairs={{1,0},{2,1},{3,2},{5,4},{6,5},{7,6},{9,8},{10,9},{11,10},{13,12},{... | collective-permute-start | bytes 110600 | tf_op jit(solution)/shard_map/ppermute | solution.py:21
  97.7 1.3 copy-start.11
  98.5 8.1 %copy-start.2 = (bf16[1,2,48,384]{3,2,1,0:T(8,128)(2,1)S(1)}, bf16[1,2,48,384]{3,2,1,0:T(8,128)(2,1)}, u32[]{:S(2)}) copy-start(bf16[1,2,48,384]{3,2,1,0:T(8,128)(2,1)} %param.15) | copy-start | bytes 221188
  98.9 27.3 %copy-start.8 = (f32[384]{0:T(512)S(1)}, f32[384]{0:T(512)}, u32[]{:S(2)}) copy-start(f32[384]{0:T(512)} %param.25) | copy-start | bytes 4612
  99.0 27.3 %copy-start.9 = (f32[384]{0:T(512)S(1)}, f32[384]{0:T(512)}, u32[]{:S(2)}) copy-start(f32[384]{0:T(512)} %param.24) | copy-start | bytes 4612
  99.0 27.4 %copy-start.3 = (bf16[384,384]{1,0:T(8,128)(2,1)S(1)}, bf16[384,384]{1,0:T(8,128)(2,1)}, u32[]{:S(2)}) copy-start(bf16[384,384]{1,0:T(8,128)(2,1)} %param.27) | copy-start | bytes 884740
  106.3 35.6 %copy-start.4 = (bf16[384,384]{1,0:T(8,128)(2,1)S(1)}, bf16[384,384]{1,0:T(8,128)(2,1)}, u32[]{:S(2)}) copy-start(bf16[384,384]{1,0:T(8,128)(2,1)} %param.28) | copy-start | bytes 884740
  126.3 30.1 %copy-start.5 = (bf16[384,384]{1,0:T(8,128)(2,1)S(1)}, bf16[384,384]{1,0:T(8,128)(2,1)}, u32[]{:S(2)}) copy-start(bf16[384,384]{1,0:T(8,128)(2,1)} %param.29) | copy-start | bytes 884740
where the time goes:
time: 158 us; the launch traced here: 157 us
  blocking collectives  116 us (73%)
  local copies, waits for them, and re-layouts  12.1 us (8%)
  starting transfers between devices  10.1 us (6%)
  matrix products  9.27 us (6%)
  other arithmetic  5.53 us (4%)
  waiting for transfers between devices  3.52 us (2%)
    psum x3, blocking collectives, group_norm(): sums = lax.psum(jnp.sum(grouped, axis=(1, 2, 4)), 'rows')  32.1 us
    psum x3, blocking collectives, group_norm(): lax.psum(jnp.sum(centered * centered, axis=(1, 2, 4)), 'rows') / entries  27.3 us
    all_gather x1, blocking collectives, per_device(): lax.all_gather(keys.reshape(shape4), 'rows', axis=1, tiled=True)  14.7 us
    all_gather x2, blocking collectives, causal_conv(): clip_frames = lax.all_gather(widened, 'tm', axis=0, tiled=True)  14.4 us
    all_gather x1, blocking collectives, per_device(): lax.all_gather(values.reshape(shape4), 'rows', axis=1, tiled=True)  14.1 us
    all_to_all x2, blocking collectives, causal_conv(): lax.all_to_all(result, 'tm', split_axis=1, concat_axis=0, tiled=True)  13.4 us
    ppermute x2, starting transfers between devices, extended(): lax.ppermute(tail, axis, [(i, (i + 1) % count) for i in range(ends)])  7.47 us
    dot_general x18, matrix products, causal_conv(): lax.dot_general(tap_weight, stacked.reshape(-1, 3 * channels), (((1,), (1...  7.32 us
  transfers between devices with their start and end apart: 4, of which 2 were waited for; matrix products, arithmetic and copies ran while one was open for 3% of the time, Pallas kernels for 0%

commit v1 on v0

--- a/solution.py
+++ b/solution.py
@@ -63,7 +63,18 @@
         .astype(jnp.bfloat16)
         .reshape(outputs, frame_count, row_count, col_count)
     )
-    mixed = lax.all_to_all(result, "tm", split_axis=1, concat_axis=0, tiled=True)
+    ways, here = (lax.axis_size("tm"), lax.axis_index("tm"))
+    width_2 = result.shape[1] // ways
+    dims = list(result.shape)
+    dims[1] = width_2
+    height = dims[0]
+    dims[0] = height * ways
+    mixed = jnp.zeros(dims, result.dtype)
+    for mask in range(ways):
+        part = lax.dynamic_slice_in_dim(result, (here ^ mask) * width_2, width_2, axis=1)
+        if mask:
+            part = lax.ppermute(part, "tm", [(d, d ^ mask) for d in range(ways)])
+        mixed = lax.dynamic_update_slice_in_dim(mixed, part, (here ^ mask) * height, axis=0)
     return jnp.transpose(mixed, (1, 2, 3, 0))
 
 

time: 158 us -> 155 us (0.981)
  blocking collectives: 116 us -> 102 us
  starting transfers between devices: 10.1 us -> 14 us
  waiting for transfers between devices: 3.52 us -> 6.85 us
  local copies, waits for them, and re-layouts: 12.1 us -> 15.2 us
    all_to_all x2 -> x0, blocking collectives: 13.4 us -> none  [causal_conv(): lax.all_to_all(result, 'tm', split_axis=1, concat_axis=0, tiled=True)]
    ppermute x0 -> x6, starting transfers between devices: none -> 3.85 us  [causal_conv(): part = lax.ppermute(part, 'tm', [(d, d ^ mask) for d in range(ways)])]
    dynamic_update_slice x0 -> x8, local copies, waits for them, and re-layouts: none -> 3.5 us  [causal_conv(): lax.dynamic_update_slice_in_dim(mixed, part, (here ^ mask) * height, axis=0)]
    ppermute x0 -> x6, waiting for transfers between devices: none -> 3.4 us  [causal_conv(): part = lax.ppermute(part, 'tm', [(d, d ^ mask) for d in range(ways)])]
  transfers between devices with their start and end apart: 4 -> 10, of which waited for: 2 -> 5; matrix products, arithmetic and copies ran while one was open for 3% -> 5% of each run, Pallas kernels for 0% -> 0%
where the time goes in v1:
time: 155 us; the launch traced here: 154 us
  blocking collectives  102 us (66%)
  local copies, waits for them, and re-layouts  15.2 us (10%)
  starting transfers between devices  14 us (9%)
  matrix products  9.27 us (6%)
  waiting for transfers between devices  6.85 us (4%)
  other arithmetic  5.51 us (4%)
    psum x3, blocking collectives, group_norm(): sums = lax.psum(jnp.sum(grouped, axis=(1, 2, 4)), 'rows')  32.2 us
    psum x3, blocking collectives, group_norm(): lax.psum(jnp.sum(centered * centered, axis=(1, 2, 4)), 'rows') / entries  27.4 us
    all_gather x2, blocking collectives, causal_conv(): clip_frames = lax.all_gather(widened, 'tm', axis=0, tiled=True)  14.7 us
    all_gather x1, blocking collectives, per_device(): lax.all_gather(keys.reshape(shape4), 'rows', axis=1, tiled=True)  14.1 us
    all_gather x1, blocking collectives, per_device(): lax.all_gather(values.reshape(shape4), 'rows', axis=1, tiled=True)  13.9 us
    ppermute x2, starting transfers between devices, extended(): lax.ppermute(tail, axis, [(i, (i + 1) % count) for i in range(ends)])  7.55 us
    dot_general x18, matrix products, causal_conv(): lax.dot_general(tap_weight, stacked.reshape(-1, 3 * channels), (((1,), (1...  7.33 us
    slice x20, local copies, waits for them, and re-layouts, causal_conv(): tap_weight = kernel[:, tap_time, tap_row].reshape(outputs, 3 * channels)  4.82 us
  transfers between devices with their start and end apart: 10, of which 5 were waited for; matrix products, arithmetic and copies ran while one was open for 5% of the time, Pallas kernels for 0%

profile of v1, /device:TPU:0, one launch (start us, length us, event | category | flops | bytes accessed | tf_op | source)
XLA Modules:
  0.0 154.1 jit_solution(6354996630325969175)
XLA Ops:
  0.0 1.0 convert_reduce_fusion.1
  1.2 13.5 %psum.42 = f32[1,32]{1,0:T(1,128)S(1)} all-reduce(f32[1,32]{1,0:T(1,128)S(1)} %bitcast.262), channel_id=1, replica_groups=mesh['clips'=2,'tm'=4,'rows'=4] {'rows'}, use_global_device_ids=true, to_apply=%region_2.0 | all-reduce | flops 32 | bytes 256 | tf_op jit(solution)/shard_map/psum | solution.py:32
  14.8 0.9 fusion.23
  16.0 8.4 %psum.43 = f32[1,32]{1,0:T(1,128)S(1)} all-reduce(f32[1,32]{1,0:T(1,128)S(1)} %bitcast.263), channel_id=1, replica_groups=mesh['clips'=2,'tm'=4,'rows'=4] {'rows'}, use_global_device_ids=true, to_apply=%region_5.6 | all-reduce | flops 32 | bytes 256 | tf_op jit(solution)/shard_map/psum | solution.py:35
  24.5 1.0 fusion.31
  25.5 3.9 %collective-permute-start = (bf16[1,1,48,384]{3,2,1,0:T(8,128)(2,1)S(1)}, bf16[1,1,48,384]{3,2,1,0:T(8,128)(2,1)S(1)}, u32[]{:S(2)}, u32[]{:S(2)}) collective-permute-start(bf16[1,1,48,384]{3,2,1,0:T(8,128)(2,1)S(1)} %get-tuple-element.89), channel_id=1, source_target_pairs={{0,1},{1,2},{2,3},{4,5},{5,6},{6,7},{8,9},{9,10},{10,11},{12,13},{... | collective-permute-start | bytes 110600 | tf_op jit(solution)/shard_map/ppermute | solution.py:19
  29.4 1.3 collective-permute-start.1
  30.7 1.8 %fusion.52 = (bf16[96,1,1,3,384]{4,0,3,2,1:T(8,128)(2,1)S(1)}, bf16[96,1,1,3,384]{4,0,3,2,1:T(8,128)(2,1)S(1)}, bf16[96,1,1,3,384]{4,0,3,2,1:T(8,128)(2,1)S(1)},...) fusion(bf16[96,3,3,3,384]{4,0,3,2,1:T(8,128)(2,1)} %param.18), kind=kLoop, calls=%fused_computation.162 | loop fusion | bytes 3981312 | tf_op jit(solution)/shard_map/slice | solution.py:54
  34.4 0.9 collective-permute-done.1
  35.3 7.5 %all_gather.12 = bf16[4,4,48,384]{3,2,1,0:T(8,128)(2,1)S(1)} all-gather(bf16[1,4,48,384]{3,2,1,0:T(8,128)(2,1)S(1)} %pad_maximum_fusion.18), channel_id=1, replica_groups=mesh['clips'=2,'tm'=4,'rows'=4] {'tm'}, dimensions={0}, use_global_device_ids=true | all-gather | bytes 737280 | tf_op jit(solution)/shard_map/all_gather | solution.py:42
  42.8 1.8 %pad_slice_fusion.25 = (bf16[4,2,48,384]{3,2,1,0:T(8,128)(2,1)S(1)}, bf16[4,2,48,384]{3,2,1,0:T(8,128)(2,1)S(1)}, bf16[4,2,48,384]{3,2,1,0:T(8,128)(2,1)S(1)}, b...) fusion(bf16[4,4,48,384]{3,2,1,0:T(8,128)(2,1)S(1)} %all_gather.12), kind=kLoop, calls=%fused_computation.25 | loop fusion | bytes 6193152 | tf_op jit(solution)/shard_map/slice | solution.py:52
  50.2 0.7 collective-permute-start.3
  50.8 0.8 collective-permute-start.4
  51.9 0.5 dynamic_update_slice.25
  52.5 1.7 %collective-permute-done.3 = bf16[96,1,2,48]{0,3,2,1:T(8,128)(2,1)S(1)} collective-permute-done((bf16[96,1,2,48]{0,3,2,1:T(8,128)(2,1)S(1)}, bf16[96,1,2,48]{0,3,2,1:T(8,128)(2,1)S(1)}, u32[]{:S(2)}, u32[]{:S(2)}) %collective-permute-start.3) | collective-permute-done | bytes 18464 | tf_op jit(solution)/shard_map/ppermute | solution.py:76
  54.2 0.5 dynamic_update_slice.26
  54.7 0.5 dynamic_update_slice.27
  55.4 10.2 %psum.44 = f32[1,32]{1,0:T(1,128)S(1)} all-reduce(f32[1,32]{1,0:T(1,128)S(1)} %bitcast.264), channel_id=1, replica_groups=mesh['clips'=2,'tm'=4,'rows'=4] {'rows'}, use_global_device_ids=true, to_apply=%region_8.9 | all-reduce | flops 32 | bytes 256 | tf_op jit(solution)/shard_map/psum | solution.py:32
  66.1 8.6 %psum.45 = f32[1,32]{1,0:T(1,128)S(1)} all-reduce(f32[1,32]{1,0:T(1,128)S(1)} %bitcast.265), channel_id=1, replica_groups=mesh['clips'=2,'tm'=4,'rows'=4] {'rows'}, use_global_device_ids=true, to_apply=%region_11.12 | all-reduce | flops 32 | bytes 256 | tf_op jit(solution)/shard_map/psum | solution.py:35
  75.0 3.7 %collective-permute-start.5 = (bf16[1,1,48,384]{3,2,1,0:T(8,128)(2,1)S(1)}, bf16[1,1,48,384]{3,2,1,0:T(8,128)(2,1)S(1)}, u32[]{:S(2)}, u32[]{:S(2)}) collective-permute-start(bf16[1,1,48,384]{3,2,1,0:T(8,128)(2,1)S(1)} %get-tuple-element.87), channel_id=1, source_target_pairs={{0,1},{1,2},{2,3},{4,5},{5,6},{6,7},{8,9},{9,10},{10,11},{12,13},{... | collective-permute-start | bytes 110600 | tf_op jit(solution)/shard_map/ppermute | solution.py:19
  78.6 1.3 collective-permute-start.6
  81.9 2.5 %collective-permute-done.6 = bf16[1,1,48,384]{3,2,1,0:T(8,128)(2,1)S(1)} collective-permute-done((bf16[1,1,48,384]{3,2,1,0:T(8,128)(2,1)S(1)}, bf16[1,1,48,384]{3,2,1,0:T(8,128)(2,1)S(1)}, u32[]{:S(2)}, u32[]{:S(2)}) %collective-permute-start.6) | collective-permute-done | bytes 36896 | tf_op jit(solution)/shard_map/ppermute | solution.py:21
  84.5 7.2 %all_gather.13 = bf16[4,4,48,384]{3,2,1,0:T(8,128)(2,1)S(1)} all-gather(bf16[1,4,48,384]{3,2,1,0:T(8,128)(2,1)S(1)} %pad_maximum_fusion.19), channel_id=1, replica_groups=mesh['clips'=2,'tm'=4,'rows'=4] {'tm'}, dimensions={0}, use_global_device_ids=true | all-gather | bytes 737280 | tf_op jit(solution)/shard_map/all_gather | solution.py:42
  91.7 1.7 %pad_slice_fusion.1 = (bf16[4,2,48,384]{3,2,1,0:T(8,128)(2,1)S(1)}, bf16[4,2,48,384]{3,2,1,0:T(8,128)(2,1)S(1)}, bf16[4,2,48,384]{3,2,1,0:T(8,128)(2,1)S(1)}, bf...) fusion(bf16[4,4,48,384]{3,2,1,0:T(8,128)(2,1)S(1)} %all_gather.13), kind=kLoop, calls=%fused_computation.1 | loop fusion | bytes 6193152 | tf_op jit(solution)/shard_map/slice | solution.py:52
  98.9 1.1 collective-permute-start.8
  100.7 0.5 dynamic_update_slice.29
  101.2 1.5 collective-permute-done.8
  104.2 8.5 %psum.46 = f32[1,32]{1,0:T(1,128)S(1)} all-reduce(f32[1,32]{1,0:T(1,128)S(1)} %bitcast.266), channel_id=1, replica_groups=mesh['clips'=2,'tm'=4,'rows'=4] {'rows'}, use_global_device_ids=true, to_apply=%region_14.15 | all-reduce | flops 32 | bytes 256 | tf_op jit(solution)/shard_map/psum | solution.py:32
  113.2 10.5 %psum.47 = f32[1,32]{1,0:T(1,128)S(1)} all-reduce(f32[1,32]{1,0:T(1,128)S(1)} %bitcast.261), channel_id=1, replica_groups=mesh['clips'=2,'tm'=4,'rows'=4] {'rows'}, use_global_device_ids=true, to_apply=%region_17.18 | all-reduce | flops 32 | bytes 256 | tf_op jit(solution)/shard_map/psum | solution.py:35
  124.1 14.1 %all_gather.14 = bf16[1,8,48,384]{3,2,0,1:T(8,128)(2,1)S(1)} all-gather(bf16[1,2,48,384]{3,2,0,1:T(8,128)(2,1)S(1)} %bitcast.259), channel_id=1, replica_groups=mesh['clips'=2,'tm'=4,'rows'=4] {'rows'}, dimensions={1}, use_global_device_ids=true | all-gather | bytes 368640 | tf_op jit(solution)/shard_map/all_gather | solution.py:142
  139.1 13.9 %all_gather.15 = bf16[1,8,48,384]{3,2,0,1:T(8,128)(2,1)S(1)} all-gather(bf16[1,2,48,384]{3,2,0,1:T(8,128)(2,1)S(1)} %bitcast.258), channel_id=1, replica_groups=mesh['clips'=2,'tm'=4,'rows'=4] {'rows'}, dimensions={1}, use_global_device_ids=true | all-gather | bytes 368640 | tf_op jit(solution)/shard_map/all_gather | solution.py:145
  153.2 0.8 fusion.4
  (160 shorter events, 20.3 us)
Async XLA Ops:
  0.0 138.2 %copy-start = (bf16[384,384]{1,0:T(8,128)(2,1)S(1)}, bf16[384,384]{1,0:T(8,128)(2,1)}, u32[]{:S(2)}) copy-start(bf16[384,384]{1,0:T(8,128)(2,1)} %param.26) | copy-start | bytes 884740
  25.5 8.8 %collective-permute-start = (bf16[1,1,48,384]{3,2,1,0:T(8,128)(2,1)S(1)}, bf16[1,1,48,384]{3,2,1,0:T(8,128)(2,1)S(1)}, u32[]{:S(2)}, u32[]{:S(2)}) collective-permute-start(bf16[1,1,48,384]{3,2,1,0:T(8,128)(2,1)S(1)} %get-tuple-element.89), channel_id=1, source_target_pairs={{0,1},{1,2},{2,3},{4,5},{5,6},{6,7},{8,9},{9,10},{10,11},{12,13},{... | collective-permute-start | bytes 110600 | tf_op jit(solution)/shard_map/ppermute | solution.py:19
  29.4 5.9 %collective-permute-start.1 = (bf16[1,1,48,384]{3,2,1,0:T(8,128)(2,1)S(1)}, bf16[1,1,48,384]{3,2,1,0:T(8,128)(2,1)S(1)}, u32[]{:S(2)}, u32[]{:S(2)}) collective-permute-start(bf16[1,1,48,384]{3,2,1,0:T(8,128)(2,1)S(1)} %get-tuple-element.90), channel_id=1, source_target_pairs={{1,0},{2,1},{3,2},{5,4},{6,5},{7,6},{9,8},{10,9},{11,10},{13,12},{... | collective-permute-start | bytes 110600 | tf_op jit(solution)/shard_map/ppermute | solution.py:21
  48.5 0.7 copy-start.10
  48.6 26.2 %copy-start.6 = (f32[384]{0:T(512)S(1)}, f32[384]{0:T(512)}, u32[]{:S(2)}) copy-start(f32[384]{0:T(512)} %param.21) | copy-start | bytes 4612
  48.6 26.2 %copy-start.7 = (f32[384]{0:T(512)S(1)}, f32[384]{0:T(512)}, u32[]{:S(2)}) copy-start(f32[384]{0:T(512)} %param.20) | copy-start | bytes 4612
  48.6 31.3 %copy-start.1 = (bf16[96,3,3,3,384]{4,0,3,2,1:T(8,128)(2,1)S(1)}, bf16[96,3,3,3,384]{4,0,3,2,1:T(8,128)(2,1)}, u32[]{:S(2)}) copy-start(bf16[96,3,3,3,384]{4,0,3,2,1:T(8,128)(2,1)} %param.22) | copy-start | bytes 5971972
  49.7 2.2 %collective-permute-start.2 = (bf16[96,1,2,48]{0,3,2,1:T(8,128)(2,1)S(1)}, bf16[96,1,2,48]{0,3,2,1:T(8,128)(2,1)S(1)}, u32[]{:S(2)}, u32[]{:S(2)}) collective-permute-start(bf16[96,1,2,48]{0,3,2,1:T(8,128)(2,1)S(1)} %get-tuple-element.85), channel_id=1, source_target_pairs={{0,4},{4,0},{8,12},{12,8},{1,5},{5,1},{9,13},{13,9},{2,6},{6,2},{1... | collective-permute-start | bytes 55304 | tf_op jit(solution)/shard_map/ppermute | solution.py:76
  50.2 4.0 %collective-permute-start.3 = (bf16[96,1,2,48]{0,3,2,1:T(8,128)(2,1)S(1)}, bf16[96,1,2,48]{0,3,2,1:T(8,128)(2,1)S(1)}, u32[]{:S(2)}, u32[]{:S(2)}) collective-permute-start(bf16[96,1,2,48]{0,3,2,1:T(8,128)(2,1)S(1)} %get-tuple-element.84), channel_id=1, source_target_pairs={{0,8},{4,12},{8,0},{12,4},{1,9},{5,13},{9,1},{13,5},{2,10},{6,14},... | collective-permute-start | bytes 55304 | tf_op jit(solution)/shard_map/ppermute | solution.py:76
  50.8 3.9 %collective-permute-start.4 = (bf16[96,1,2,48]{0,3,2,1:T(8,128)(2,1)S(1)}, bf16[96,1,2,48]{0,3,2,1:T(8,128)(2,1)S(1)}, u32[]{:S(2)}, u32[]{:S(2)}) collective-permute-start(bf16[96,1,2,48]{0,3,2,1:T(8,128)(2,1)S(1)} %get-tuple-element.83), channel_id=1, source_target_pairs={{0,12},{4,8},{8,4},{12,0},{1,13},{5,9},{9,5},{13,1},{2,14},{6,10},... | collective-permute-start | bytes 55304 | tf_op jit(solution)/shard_map/ppermute | solution.py:76
  75.0 7.0 %collective-permute-start.5 = (bf16[1,1,48,384]{3,2,1,0:T(8,128)(2,1)S(1)}, bf16[1,1,48,384]{3,2,1,0:T(8,128)(2,1)S(1)}, u32[]{:S(2)}, u32[]{:S(2)}) collective-permute-start(bf16[1,1,48,384]{3,2,1,0:T(8,128)(2,1)S(1)} %get-tuple-element.87), channel_id=1, source_target_pairs={{0,1},{1,2},{2,3},{4,5},{5,6},{6,7},{8,9},{9,10},{10,11},{12,13},{... | collective-permute-start | bytes 110600 | tf_op jit(solution)/shard_map/ppermute | solution.py:19
  78.6 5.9 %collective-permute-start.6 = (bf16[1,1,48,384]{3,2,1,0:T(8,128)(2,1)S(1)}, bf16[1,1,48,384]{3,2,1,0:T(8,128)(2,1)S(1)}, u32[]{:S(2)}, u32[]{:S(2)}) collective-permute-start(bf16[1,1,48,384]{3,2,1,0:T(8,128)(2,1)S(1)} %get-tuple-element.88), channel_id=1, source_target_pairs={{1,0},{2,1},{3,2},{5,4},{6,5},{7,6},{9,8},{10,9},{11,10},{13,12},{... | collective-permute-start | bytes 110600 | tf_op jit(solution)/shard_map/ppermute | solution.py:21
  96.6 1.3 copy-start.11
  97.4 6.5 %copy-start.2 = (bf16[1,2,48,384]{3,2,1,0:T(8,128)(2,1)S(1)}, bf16[1,2,48,384]{3,2,1,0:T(8,128)(2,1)}, u32[]{:S(2)}) copy-start(bf16[1,2,48,384]{3,2,1,0:T(8,128)(2,1)} %param.15) | copy-start | bytes 221188
  97.4 26.4 %copy-start.8 = (f32[384]{0:T(512)S(1)}, f32[384]{0:T(512)}, u32[]{:S(2)}) copy-start(f32[384]{0:T(512)} %param.25) | copy-start | bytes 4612
  97.5 26.4 %copy-start.9 = (f32[384]{0:T(512)S(1)}, f32[384]{0:T(512)}, u32[]{:S(2)}) copy-start(f32[384]{0:T(512)} %param.24) | copy-start | bytes 4612
  97.5 26.4 %copy-start.3 = (bf16[384,384]{1,0:T(8,128)(2,1)S(1)}, bf16[384,384]{1,0:T(8,128)(2,1)}, u32[]{:S(2)}) copy-start(bf16[384,384]{1,0:T(8,128)(2,1)} %param.27) | copy-start | bytes 884740
  98.3 40.5 %copy-start.4 = (bf16[384,384]{1,0:T(8,128)(2,1)S(1)}, bf16[384,384]{1,0:T(8,128)(2,1)}, u32[]{:S(2)}) copy-start(bf16[384,384]{1,0:T(8,128)(2,1)} %param.28) | copy-start | bytes 884740
  98.5 2.2 %collective-permute-start.7 = (bf16[96,1,2,48]{0,3,2,1:T(8,128)(2,1)S(1)}, bf16[96,1,2,48]{0,3,2,1:T(8,128)(2,1)S(1)}, u32[]{:S(2)}, u32[]{:S(2)}) collective-permute-start(bf16[96,1,2,48]{0,3,2,1:T(8,128)(2,1)S(1)} %get-tuple-element.81), channel_id=1, source_target_pairs={{0,4},{4,0},{8,12},{12,8},{1,5},{5,1},{9,13},{13,9},{2,6},{6,2},{1... | collective-permute-start | bytes 55304 | tf_op jit(solution)/shard_map/ppermute | solution.py:76
  98.9 3.8 %collective-permute-start.8 = (bf16[96,1,2,48]{0,3,2,1:T(8,128)(2,1)S(1)}, bf16[96,1,2,48]{0,3,2,1:T(8,128)(2,1)S(1)}, u32[]{:S(2)}, u32[]{:S(2)}) collective-permute-start(bf16[96,1,2,48]{0,3,2,1:T(8,128)(2,1)S(1)} %get-tuple-element.80), channel_id=1, source_target_pairs={{0,8},{4,12},{8,0},{12,4},{1,9},{5,13},{9,1},{13,5},{2,10},{6,14},... | collective-permute-start | bytes 55304 | tf_op jit(solution)/shard_map/ppermute | solution.py:76
  100.0 3.5 %collective-permute-start.9 = (bf16[96,1,2,48]{0,3,2,1:T(8,128)(2,1)S(1)}, bf16[96,1,2,48]{0,3,2,1:T(8,128)(2,1)S(1)}, u32[]{:S(2)}, u32[]{:S(2)}) collective-permute-start(bf16[96,1,2,48]{0,3,2,1:T(8,128)(2,1)S(1)} %get-tuple-element.79), channel_id=1, source_target_pairs={{0,12},{4,8},{8,4},{12,0},{1,13},{5,9},{9,5},{13,1},{2,14},{6,10},... | collective-permute-start | bytes 55304 | tf_op jit(solution)/shard_map/ppermute | solution.py:76
  123.9 29.3 %copy-start.5 = (bf16[384,384]{1,0:T(8,128)(2,1)S(1)}, bf16[384,384]{1,0:T(8,128)(2,1)}, u32[]{:S(2)}) copy-start(bf16[384,384]{1,0:T(8,128)(2,1)} %param.29) | copy-start | bytes 884740
